TPU v7x, 256 devices: a whole 4x4x8 slice. The times are simulated.
256 devices in a mesh: wave: 64 (over x, z, core), lev: 4 (over y).
Axes of the slice: x: 4, y: 4, z: 8, core: 2. Of those that a mesh axis runs over, the one named last changes fastest.
Arguments:
- spectra: bfloat16 [640, 2, 3, 128, 640], P('wave', None, None, 'lev'), may hold values from -0.15625 to 0.15625
- legendre_table: bfloat16 [640, 640, 512], P('wave'), may hold values from -0.25 to 0.25
- m_order: int32 [640], replicated, may hold values from 0 to 639, as said below
- row_points: int32 [512], replicated, may hold values from 20 to 2576, as said below
Outputs:
- grid: bfloat16 [512, 3, 128, 2688], P(('wave', 'lev'))
Inputs may be any that keep to these rules, and one draw needn't show every extreme that they name: `m_order`: A permutation of 0 to 639. Entries 2 i and 2 i + 1 are a and 639 - a with a < 320. `row_points`: each is 20 + 4 min(i, 1279 - i) for the row's latitude index i from the pole; some row lies at the equator.
All inputs are finite; a program needn't handle non-finite values.
Results may differ from a plain program's by a relative error of at most 0.0055.
Values may be sent and summed in bfloat16 or wider, within the bound.
A program may use at most 128 MiB of HBM per device.

v0:
```python
import math

import jax
import jax.numpy as jnp
from jax import lax
from jax.sharding import PartitionSpec as P

ROWPAD = 2688


def synthesis_basis(wavenumbers, points, width):
    column = wavenumbers[:, None]
    longitude = lax.iota(jnp.int32, width)[None, :]
    residue = column * longitude % points
    folded = jnp.minimum(residue, points - residue)
    angle = folded.astype(jnp.float32) * (2.0 * math.pi) / points.astype(jnp.float32)
    orient = jnp.where(2 * residue <= points, 1.0, -1.0).astype(jnp.float32)
    active = (2 * column < points) & (longitude < points)
    factor = jnp.where(active, jnp.where(column == 0, 1.0, 2.0), 0.0).astype(jnp.float32)
    cosine = (factor * jnp.cos(angle)).astype(jnp.bfloat16)
    sine = (-(factor * orient) * jnp.sin(angle)).astype(jnp.bfloat16)
    return (cosine, sine)


def trim_spectra(spectra, wavenumbers):
    degree = lax.iota(jnp.int32, spectra.shape[-1])
    keep = degree[None, :] < (spectra.shape[-1] - wavenumbers)[:, None]
    return jnp.where(keep[:, None, None, None, :], spectra, jnp.zeros((), spectra.dtype))


def contract_first(left, right):
    return lax.dot_general(
        left, right, (((0,), (0,)), ((), ())), preferred_element_type=jnp.float32
    )


def synthesize(coeffs, wavenumbers, points, width):
    row_count, halves, waves, fields, levels = coeffs.shape
    flat = coeffs.reshape(row_count, halves * waves, fields * levels)

    def one_row(pair):
        block, count = pair
        cosine, sine = synthesis_basis(wavenumbers, count, width)
        field = contract_first(block, jnp.concatenate([cosine, sine], axis=0))
        return field.astype(jnp.bfloat16).reshape(fields, levels, width)

    return lax.map(one_row, (flat, points))


def shards(spectra, legendre_table, m_order, row_points):
    local_waves = spectra.shape[0]
    owned = lax.dynamic_slice_in_dim(m_order, lax.axis_index("wave") * local_waves, local_waves)
    trimmed = trim_spectra(spectra, owned)
    coeffs = jnp.einsum(
        "mcflk,mkj->jcmfl", trimmed, legendre_table, preferred_element_type=jnp.float32
    )
    coeffs = coeffs.astype(jnp.bfloat16)
    gathered = lax.all_to_all(
        lax.all_to_all(coeffs, "wave", split_axis=0, concat_axis=2, tiled=True),
        "lev",
        split_axis=0,
        concat_axis=4,
        tiled=True,
    )
    row_count = gathered.shape[0]
    first_row = (lax.axis_index("wave") * lax.axis_size("lev") + lax.axis_index("lev")) * row_count
    points = lax.dynamic_slice_in_dim(row_points, first_row, row_count)
    return synthesize(gathered, m_order, points, ROWPAD)


def solution(mesh):
    in_specs = (P("wave", None, None, "lev", None), P("wave", None, None), P(), P())
    out_specs = P(("wave", "lev"), None, None, None)
    return jax.shard_map(shards, mesh=mesh, in_specs=in_specs, out_specs=out_specs, check_vma=False)
```

profile of v0, /device:TPU:1, one launch (start us, length us, event | category | flops | bytes accessed | tf_op | source)
XLA Modules:
  0.0 377.0 jit_solution(8572526864640914881)
XLA Ops:
  0.0 0.8 dynamic-slice_subtract_fusion
  0.8 0.1 iota_compare_fusion.1
  0.8 5.3 %convert_bitcast_fusion = bf16[512,2,10,3,32]{0,4,3,1,2:T(8,128)(2,1)S(1)} fusion(bf16[10,640,512]{2,1,0:T(8,128)(2,1)} %param.7, bf16[10,2,3,32,640]{4,3,2,1,0:T(8,128)(2,1)} %param.6, pred[10,640]{1,0:T(8,128)(4,1)S(1)} %iota_compare_fusion.1), kind=kOutput, calls=%fused_computation.35 | convolution fusion | flops 1260503040 | bytes 10983680 | tf_op jit(solution)/shard_map/mcflk,mkj->jcmfl/dot_general | solution.py:54
  6.2 12.0 %copy.16 = bf16[512,2,10,3,32]{4,1,3,2,0:T(2,128)(2,1)} copy(bf16[512,2,10,3,32]{0,4,3,1,2:T(8,128)(2,1)S(1)} %convert_bitcast_fusion) | data formatting | bytes 3932160 | tf_op jit(solution)/shard_map/convert_element_type | solution.py:57
  18.1 16.1 %reshape.43 = bf16[64,2,7680]{2,1,0:T(2,128)(2,1)S(1)} reshape(bf16[512,10,3,2,32]{4,3,2,1,0:T(2,128)(2,1)} %bitcast.35) | data formatting | bytes 3932160
  34.3 61.1 %all_to_all.33 = bf16[64,2,7680]{2,1,0:T(2,128)(2,1)} all-to-all(bf16[64,2,7680]{2,1,0:T(2,128)(2,1)S(1)} %reshape.43), channel_id=1, replica_groups=mesh['wave'=64,'lev'=4] {'wave'}, dimensions={0} | all-to-all | bytes 3932160 | tf_op jit(solution)/shard_map/all_to_all | solution.py:59
  95.4 17.3 %reshape.44 = bf16[512,10,3,2,32]{4,3,2,1,0:T(2,128)(2,1)} reshape(bf16[64,2,7680]{2,1,0:T(2,128)(2,1)} %all_to_all.33) | data formatting | bytes 3932160
  112.7 5.2 %copy.25 = bf16[512,2,10,3,32]{4,0,3,2,1:T(8,128)(2,1)S(1)} copy(bf16[512,2,10,3,32]{4,1,3,2,0:T(2,128)(2,1)} %bitcast.36) | data formatting | bytes 3932160 | tf_op jit(solution)/shard_map/all_to_all | solution.py:59
  117.9 4.4 %copy.18 = bf16[8,2,64,10,3,32]{5,0,4,3,2,1:T(8,128)(2,1)} copy(bf16[8,2,64,10,3,32]{5,0,2,4,3,1:T(8,128)(2,1)S(1)} %bitcast.37) | data formatting | bytes 3932160 | tf_op jit(solution)/shard_map/all_to_all | solution.py:59
  122.3 10.1 %copy.19 = bf16[8,2,640,3,32]{2,4,3,1,0:T(8,128)(2,1)} copy(bf16[8,2,640,3,32]{4,0,3,2,1:T(8,128)(2,1)} %bitcast.38) | data formatting | bytes 3932160 | tf_op jit(solution)/shard_map/all_to_all | solution.py:59
  132.4 4.2 %all-to-all-start.1 = ((bf16[8,2,640,3,32]{2,4,3,1,0:T(8,128)(2,1)}), bf16[8,2,640,3,32]{2,4,3,1,0:T(8,128)(2,1)S(1)}, u32[]{:S(2)}, u32[]{:S(2)}) async-start(bf16[8,2,640,3,32]{2,4,3,1,0:T(8,128)(2,1)} %copy.19), calls=%async_computation.1 | async-start | bytes 3932160 | tf_op jit(solution)/shard_map/all_to_all | solution.py:58
  136.6 0.0 copy-start
  136.6 0.8 dynamic_slice.15
  137.4 23.5 %all-to-all-done.1 = bf16[8,2,640,3,32]{2,4,3,1,0:T(8,128)(2,1)S(1)} async-done(((bf16[8,2,640,3,32]{2,4,3,1,0:T(8,128)(2,1)}), bf16[8,2,640,3,32]{2,4,3,1,0:T(8,128)(2,1)S(1)}, u32[]{:S(2)}, u32[]{:S(2)}) %all-to-all-start.1) | async-done | bytes 1966112 | tf_op jit(solution)/shard_map/all_to_all | solution.py:58
  160.9 3.2 copy.20
  164.1 4.6 %reshape.41 = bf16[2,1280,384]{1,2,0:T(8,128)(2,1)S(1)} reshape(bf16[2,2,640,3,4,32]{2,1,5,4,3,0:T(2,128)(2,1)} %copy.20) | data formatting | bytes 3932160 | tf_op jit(solution)/shard_map/reshape | solution.py:39
  168.7 0.0 copy-done
  168.8 208.3 %while.10 = (s32[]{:T(128)}, bf16[2,3,128,2688]{3,2,1,0:T(8,128)(2,1)}, bf16[2,1280,384]{1,2,0:T(8,128)(2,1)S(1)}, s32[640]{0:T(1024)S(1)}, s32[2]{0:T(128)S(1)}, /*index=5*/s32[]{:T(128)}, s32[]{:T(128)}) while((s32[]{:T(128)}, bf16[2,3,128,2688]{3,2,1,0:T(8,128)(2,1)}, bf16[2,1280,384]{1,2,0:T(8,128)(2,1)S(1)}, s32[640]{0:T(1024)S(1)}, ...), condition=%wide.region_1.2_spmd, body=%wide.region_0.1_spmd.sunk | while | flops 2698499328 | bytes 20958872 | solution.py:47
  168.8 0.6 dynamic_slice.24
  170.6 0.6 multiply_compare_fusion.3
  171.2 0.6 iota_compare_fusion.3
  172.5 95.9 %fusion.38 = (bf16[640,2688]{1,0:T(8,128)(2,1)S(1)}, bf16[640,2688]{1,0:T(8,128)(2,1)S(1)}) fusion(f32[640]{0:T(1024)S(1)} %compare_select_fusion.2, f32[]{:T(128)S(6)} %convert_element_type.43, s32[]{:T(128)} %bitcast.32, pred[]{:T(512)S(6)} %lt.93, s32[]{:T(128)S(6)} %select_n.73, s32[640]{0:T(1024)S(1)} %get-tuple-element.112, ...), kind=kLoop, calls=%fused_computation.4.clone.1 | loop fusion | flops 41287680 | bytes 6889741 | tf_op jit(solution)/shard_map/while/body/eval_jaxpr/convert_element_type | solution.py:20
  268.4 3.0 fusion.39
  271.4 1.5 constant_dynamic-update-slice_fusion.2
  272.9 0.6 dynamic_slice.24
  274.7 0.6 multiply_compare_fusion.3
  275.4 0.6 iota_compare_fusion.3
  276.6 95.9 %fusion.38 = (bf16[640,2688]{1,0:T(8,128)(2,1)S(1)}, bf16[640,2688]{1,0:T(8,128)(2,1)S(1)}) fusion(f32[640]{0:T(1024)S(1)} %compare_select_fusion.2, f32[]{:T(128)S(6)} %convert_element_type.43, s32[]{:T(128)} %bitcast.32, pred[]{:T(512)S(6)} %lt.93, s32[]{:T(128)S(6)} %select_n.73, s32[640]{0:T(1024)S(1)} %get-tuple-element.112, ...), kind=kLoop, calls=%fused_computation.4.clone.1 | loop fusion | flops 41287680 | bytes 6889741 | tf_op jit(solution)/shard_map/while/body/eval_jaxpr/convert_element_type | solution.py:20
  372.5 3.0 fusion.39
  375.6 1.5 constant_dynamic-update-slice_fusion.2
  (3 shorter events, 0.0 us)
Async XLA Ops:
  132.4 28.5 %all-to-all-start.1 = ((bf16[8,2,640,3,32]{2,4,3,1,0:T(8,128)(2,1)}), bf16[8,2,640,3,32]{2,4,3,1,0:T(8,128)(2,1)S(1)}, u32[]{:S(2)}, u32[]{:S(2)}) async-start(bf16[8,2,640,3,32]{2,4,3,1,0:T(8,128)(2,1)} %copy.19), calls=%async_computation.1 | async-start | bytes 3932160 | tf_op jit(solution)/shard_map/all_to_all | solution.py:58
  136.6 32.2 %copy-start = (s32[640]{0:T(1024)S(1)}, s32[640]{0:T(1024)}, u32[]{:S(2)}) copy-start(s32[640]{0:T(1024)} %param.8) | copy-start | bytes 7684
where the time goes:
time: 378 us; the launch traced here: 377 us
  other arithmetic  195 us (52%)
  local copies, waits for them, and re-layouts  77.8 us (21%)
  blocking collectives  61.1 us (16%)
  waiting for transfers between devices  23.5 us (6%)
  matrix products  11.3 us (3%)
  starting transfers between devices  4.18 us (1%)
  loops' own time  3.81 us (1%)
    convert_element_type x2, other arithmetic, synthesis_basis(): cosine = (factor * jnp.cos(angle)).astype(jnp.bfloat16)  192 us
    all_to_all x1, blocking collectives, shards(): lax.all_to_all(coeffs, 'wave', split_axis=0, concat_axis=2, tiled=True)  61.1 us
    unnamed x4, local copies, waits for them, and re-layouts  33.4 us
    all_to_all x1, waiting for transfers between devices, shards(): lax.all_to_all(lax.all_to_all(coeffs, 'wave', split_axis=0, concat_axis=2...  23.5 us
    all_to_all x3, local copies, waits for them, and re-layouts, shards(): lax.all_to_all(coeffs, 'wave', split_axis=0, concat_axis=2, tiled=True)  19.7 us
    convert_element_type x1, local copies, waits for them, and re-layouts, shards(): coeffs = coeffs.astype(jnp.bfloat16)  12 us
  transfers between devices with their start and end apart: 1, of which 1 were waited for; matrix products, arithmetic and copies ran while one was open for 0% of the time, Pallas kernels for 0%

commit v1 on v0

v1 whole, which is shorter than its diff:
```python
import functools
import math

import jax
import jax.numpy as jnp
import numpy as np
from jax import lax
from jax.experimental import pallas as pl
from jax.experimental.pallas import tpu as pltpu
from jax.sharding import PartitionSpec as P

MESH = pl.DeviceIdType.MESH
NX, NY, NZ, NC = 4, 4, 8, 2
NPEER = NX * NY * NC
WAVES = 10
PAIRS = WAVES // 2
FL = 96
PAIR_LANES = 4 * FL
LANES = PAIRS * PAIR_LANES
DEG = 640
NLAT = 512
ROWPAD = 2688
TILES = ROWPAD // 128
KTOT = 1280
PARTS = ((0, 128), (128, 256), (384, 384), (768, 384), (1152, 384), (1536, 384))


def permutations():
    by_peer = np.zeros((NLAT, NLAT), np.float32)
    for x in range(NX):
        for y in range(NY):
            for c in range(NC):
                for z in range(NZ):
                    for i in range(2):
                        row = ((x * NZ + z) * NC + c) * 8 + y * 2 + i
                        by_peer[(((x * NY + y) * NC + c) * NZ + z) * 2 + i, row] = 1
    by_z = np.zeros((128, 128), np.float32)
    to_k = np.zeros((128, 256), np.float32)
    for s in range(8):
        for z in range(NZ):
            for i in range(2):
                by_z[z * 16 + i * 8 + s, s * 16 + z * 2 + i] = 1
                to_k[z * 16 + i * 8 + s, i * 64 + z * 8 + s] = 1
                to_k[z * 16 + i * 8 + s, 128 + (1 - i) * 64 + z * 8 + s] = 1
    return tuple(jnp.asarray(a, jnp.bfloat16) for a in (by_peer, by_z, to_k))


def dot(a, b, dims):
    return lax.dot_general(a, b, (dims, ((), ())), preferred_element_type=jnp.float32)


def unit_circle(wave, lon, points):
    inverse = 1.0 / points
    turns = wave * lon
    residue = turns - jnp.floor(turns * inverse) * points
    residue = jnp.where(residue < 0.0, residue + points, residue)
    residue = jnp.where(residue >= points, residue - points, residue)
    folded = jnp.minimum(residue, points - residue)
    u = (points - 4.0 * folded) * ((0.5 * math.pi) * inverse)
    v = u * u
    cosine, sine = jnp.full_like(u, 1.0 / math.factorial(13)), jnp.full_like(u, 1.0 / math.factorial(14))
    for n in range(6):
        cosine = cosine * -v + 1.0 / math.factorial(11 - 2 * n)
        sine = sine * -v + 1.0 / math.factorial(12 - 2 * n)
    sine = 1.0 - v * sine
    cosine = cosine * u
    sine = jnp.where(2.0 * residue <= points, sine, -sine)
    return cosine, sine


def move_kernel(
    m_ref, p_ref, spec_hbm, leg_hbm, by_peer_hbm, by_z_hbm, to_k_hbm,
    a_hbm, b_hbm,
    spec, leg, by_peer, by_z, to_k, coef, sent, mid, ordered, final, a_out,
    waves, cos_now, sin_now, cos_step, sin_step, b_out,
    in_sem, xy_send, xy_recv, xy_own, z_send, z_recv, z_own, a_sem, b_sem,
):
    w, y = lax.axis_index("wave"), lax.axis_index("lev")
    x, z, c = w // 16, lax.rem(w // 2, 8), lax.rem(w, 2)

    def peer(d):
        px, py, pc = lax.rem(x + d // 8, NX), lax.rem(y + lax.rem(d // 2, 4), NY), lax.rem(c + lax.rem(d, 2), NC)
        return px, py, pc

    def wave_of(px, pz, pc):
        return (px * NZ + pz) * NC + pc

    loads = [
        pltpu.make_async_copy(by_peer_hbm, by_peer, in_sem.at[0]),
        pltpu.make_async_copy(by_z_hbm, by_z, in_sem.at[1]),
        pltpu.make_async_copy(to_k_hbm, to_k, in_sem.at[2]),
    ]
    fetch = []
    for g in range(PAIRS):
        cut = pl.ds(2 * g, 2)
        fetch.append((
            pltpu.make_async_copy(spec_hbm.at[cut], spec.at[cut], in_sem.at[3 + 2 * g]),
            pltpu.make_async_copy(leg_hbm.at[cut], leg.at[cut], in_sem.at[4 + 2 * g]),
        ))
    for f in fetch[0]:
        f.start()
    for f in loads:
        f.start()
    for pair in fetch[1:]:
        for f in pair:
            f.start()

    barrier = pltpu.get_barrier_semaphore()

    @pl.loop(1, NPEER)
    def _(d):
        px, py, pc = peer(d)
        pl.semaphore_signal(barrier, inc=1, device_id=(wave_of(px, z, pc), py), device_id_type=MESH)

    @pl.loop(1, NZ)
    def _(d):
        pl.semaphore_signal(barrier, inc=1, device_id=(wave_of(x, lax.rem(z + d, NZ), c), y), device_id_type=MESH)

    for f in loads:
        f.wait()
    slot = y * 8 + x * 2 + c
    own = (x * NY + y) * NC + c

    def spectral(g):
        for f in fetch[g]:
            f.wait()
        for h in range(2):
            r = 2 * g + h
            top = DEG - m_ref[w * WAVES + r]
            degree = lax.broadcasted_iota(jnp.int32, (2 * FL, DEG), 1)
            trimmed = jnp.where(degree < top, spec[r], jnp.zeros((), jnp.bfloat16))
            coef[h * 2 * FL:(h + 1) * 2 * FL, :] = dot(trimmed, leg[r], ((1,), (0,))).astype(jnp.bfloat16)
        moved = dot(by_peer[...], coef[...], ((1,), (1,))).astype(jnp.bfloat16)
        sent[:, :, g * PAIR_LANES:(g + 1) * PAIR_LANES] = moved.reshape(NPEER, 16, PAIR_LANES)

    def send_xy(q):
        first, size = PARTS[q]
        cut = pl.ds(first, size)

        @pl.loop(1, NPEER)
        def _(d):
            px, py, pc = peer(d)
            pltpu.make_async_remote_copy(
                src_ref=sent.at[(px * NY + py) * NC + pc, :, cut],
                dst_ref=mid.at[slot, :, cut],
                send_sem=xy_send.at[q],
                recv_sem=xy_recv.at[q],
                device_id=(wave_of(px, z, pc), py),
                device_id_type=MESH,
            ).start()

        pltpu.make_async_copy(sent.at[own, :, cut], mid.at[slot, :, cut], xy_own.at[q]).start()

    def wait_xy(q):
        first, size = PARTS[q]
        cut = pl.ds(first, size)
        most = mid.at[pl.ds(0, NPEER - 1), :, cut]
        pltpu.make_async_copy(most, most, xy_recv.at[q]).wait()
        pltpu.make_async_copy(sent.at[own, :, cut], mid.at[slot, :, cut], xy_own.at[q]).wait()

    def z_copy(q, d):
        first, size = PARTS[q]
        cut = pl.ds(first, size)
        pz = lax.rem(z + d, NZ)
        return pltpu.make_async_remote_copy(
            src_ref=ordered.at[pz, :, :, cut],
            dst_ref=final.at[z, :, :, cut],
            send_sem=z_send.at[q],
            recv_sem=z_recv.at[q],
            device_id=(wave_of(x, pz, c), y),
            device_id_type=MESH,
        )

    def z_stay(q):
        first, size = PARTS[q]
        cut = pl.ds(first, size)
        return pltpu.make_async_copy(ordered.at[z, :, :, cut], final.at[z, :, :, cut], z_own.at[q])

    def send_z(q):
        first, size = PARTS[q]
        for group in range(NY):
            block = mid[group * 8:(group + 1) * 8, :, first:first + size].reshape(128, size)
            moved = dot(by_z[...], block, ((1,), (0,))).astype(jnp.bfloat16)
            ordered[:, group, :, first:first + size] = moved.reshape(NZ, 16, size)
        for d in (4, 3, 5, 2, 6, 1, 7):
            z_copy(q, d).start()
        z_stay(q).start()

    def wait_z(q):
        first, size = PARTS[q]
        most = final.at[pl.ds(0, NZ - 1), :, :, pl.ds(first, size)]
        pltpu.make_async_copy(most, most, z_recv.at[q]).wait()
        z_stay(q).wait()

    def rows_of(g):
        lane = lax.broadcasted_iota(jnp.int32, (FL, 128), 1)
        for group in range(NY):
            block = final[:, group, :, g * PAIR_LANES:(g + 1) * PAIR_LANES].reshape(128, PAIR_LANES)
            turned = dot(block, to_k[...], ((0,), (0,)))
            for h in range(2):
                real, imag = (turned[(2 * h + k) * FL:(2 * h + k + 1) * FL] for k in range(2))
                even = jnp.where(lane < 64, real[:, :128], imag[:, 128:])
                odd = jnp.where(lane < 64, imag[:, 128:], real[:, :128])
                at = (2 * g + h) * 128
                a_out[0, group * FL:(group + 1) * FL, at:at + 128] = even.astype(jnp.bfloat16)
                a_out[1, group * FL:(group + 1) * FL, at:at + 128] = odd.astype(jnp.bfloat16)

    def a_copy(g):
        cut = pl.ds(g * 256, 256)
        return pltpu.make_async_copy(a_out.at[:, :, cut], a_hbm.at[:, :, cut], a_sem.at[g])

    def b_copy(i, k, t):
        return pltpu.make_async_copy(b_out.at[k], b_hbm.at[i, :, pl.ds(pl.multiple_of(t * 128, 128), 128)], b_sem.at[k])

    def bases():
        @pl.loop(0, KTOT // 2)
        def _(k):
            block, s = k // 64, lax.rem(k, 8)
            source = wave_of(s // 2, lax.rem(k // 8, 8), lax.rem(s, 2))
            waves[pl.ds(k, 1), :] = jnp.full((1, 128), m_ref[source * WAVES + block]).astype(jnp.float32)

        for i in range(2):
            count = p_ref[(w * NY + y) * 2 + i]

            @pl.loop(0, 10)
            def _(block):
                rows = pl.ds(pl.multiple_of(block * 64, 64), 64)
                points = jnp.full((64, 128), count).astype(jnp.float32)
                wave = waves[rows, :]
                lon = lax.broadcasted_iota(jnp.int32, (64, 128), 1).astype(jnp.float32)
                cosine, sine = unit_circle(wave, lon, points)
                weight = jnp.where(2.0 * wave < points, jnp.where(wave == 0.0, 1.0, 2.0), 0.0)
                cos_now[rows, :] = weight * cosine
                sin_now[rows, :] = -weight * sine
                cosine, sine = unit_circle(wave, 128.0, points)
                cos_step[rows, :] = cosine
                sin_step[rows, :] = sine

            @pl.loop(0, TILES)
            def _(t):
                k = lax.rem(t + i * TILES, 2)

                @pl.when(t + i * TILES >= 2)
                def _():
                    b_copy(i, k, t).wait()

                for block in range(10):
                    rows = slice(block * 64, (block + 1) * 64)
                    cosine, sine, cs, ss = cos_now[rows, :], sin_now[rows, :], cos_step[rows, :], sin_step[rows, :]
                    first = block * 128 + i * 64
                    second = block * 128 + (1 - i) * 64
                    b_out[k, first:first + 64, :] = cosine.astype(jnp.bfloat16)
                    b_out[k, second:second + 64, :] = sine.astype(jnp.bfloat16)
                    cos_now[rows, :] = cosine * cs + sine * ss
                    sin_now[rows, :] = sine * cs - cosine * ss
                b_copy(i, k, t).start()

        for k in range(2):
            b_copy(1, k, 0).wait()

    spectral(0)
    pl.semaphore_wait(barrier, NPEER - 1 + NZ - 1)
    send_xy(0)
    send_xy(1)
    for g in range(1, PAIRS):
        spectral(g)
        send_xy(g + 1)
    for q in range(len(PARTS)):
        wait_xy(q)
        send_z(q)
    bases()
    for q in range(len(PARTS)):
        wait_z(q)
        if q:
            rows_of(q - 1)
            a_copy(q - 1).start()
    for g in range(PAIRS):
        a_copy(g).wait()
    for q in range(len(PARTS)):
        first, size = PARTS[q]
        most = mid.at[pl.ds(0, NPEER - 1), :, pl.ds(first, size)]
        pltpu.make_async_copy(most, most, xy_send.at[q]).wait()
        most = final.at[pl.ds(0, NZ - 1), :, :, pl.ds(first, size)]
        pltpu.make_async_copy(most, most, z_send.at[q]).wait()


def move(spectra, legendre_table, m_order, row_points):
    by_peer, by_z, to_k = permutations()
    hbm = pl.BlockSpec(memory_space=pl.ANY)
    smem = pl.BlockSpec(memory_space=pltpu.SMEM)
    n = len(PARTS)
    bf16, f32 = jnp.bfloat16, jnp.float32
    dma = pltpu.SemaphoreType.DMA
    return pl.pallas_call(
        move_kernel,
        out_shape=(
            jax.ShapeDtypeStruct((2, 4 * FL, KTOT), bf16),
            jax.ShapeDtypeStruct((2, KTOT, ROWPAD), bf16),
        ),
        in_specs=[smem, smem, hbm, hbm, hbm, hbm, hbm],
        out_specs=(hbm, hbm),
        scratch_shapes=[
            pltpu.VMEM((WAVES, 2 * FL, DEG), bf16),
            pltpu.VMEM((WAVES, DEG, NLAT), bf16),
            pltpu.VMEM((NLAT, NLAT), bf16),
            pltpu.VMEM((128, 128), bf16),
            pltpu.VMEM((128, 256), bf16),
            pltpu.VMEM((PAIR_LANES, NLAT), bf16),
            pltpu.VMEM((NPEER, 16, LANES), bf16),
            pltpu.VMEM((NPEER, 16, LANES), bf16),
            pltpu.VMEM((NZ, NY, 16, LANES), bf16),
            pltpu.VMEM((NZ, NY, 16, LANES), bf16),
            pltpu.VMEM((2, 4 * FL, KTOT), bf16),
            pltpu.VMEM((KTOT // 2, 128), f32),
            pltpu.VMEM((KTOT // 2, 128), f32),
            pltpu.VMEM((KTOT // 2, 128), f32),
            pltpu.VMEM((KTOT // 2, 128), f32),
            pltpu.VMEM((KTOT // 2, 128), f32),
            pltpu.VMEM((2, KTOT, 128), bf16),
            dma((3 + 2 * PAIRS,)),
            dma((n,)), dma((n,)), dma((n,)),
            dma((n,)), dma((n,)), dma((n,)),
            dma((PAIRS,)), dma((2,)),
        ],
        compiler_params=pltpu.CompilerParams(
            collective_id=0, has_side_effects=True, vmem_limit_bytes=56 << 20
        ),
    )(m_order, row_points, spectra, legendre_table, by_peer, by_z, to_k)


WIDTH = 384


def synth_kernel(p_ref, a_ref, b_ref, grid_ref):
    i, t = pl.program_id(0), pl.program_id(1)
    row = (lax.axis_index("wave") * NY + lax.axis_index("lev")) * 2 + i
    field = dot(a_ref[0], b_ref[0], ((1,), (0,)))
    lon = lax.broadcasted_iota(jnp.int32, (4 * FL, WIDTH), 1) + t * WIDTH
    field = jnp.where(lon < p_ref[row], field, 0.0).astype(jnp.bfloat16)
    for y in range(NY):
        for f in range(3):
            grid_ref[0, f, y * 32:(y + 1) * 32, :] = field[y * FL + f * 32:y * FL + (f + 1) * 32]


def synthesize(a, b, row_points):
    return pl.pallas_call(
        synth_kernel,
        out_shape=jax.ShapeDtypeStruct((2, 3, 128, ROWPAD), jnp.bfloat16),
        grid=(2, ROWPAD // WIDTH),
        in_specs=[
            pl.BlockSpec(memory_space=pltpu.SMEM),
            pl.BlockSpec((1, 4 * FL, KTOT), lambda i, t: (i, 0, 0)),
            pl.BlockSpec((1, KTOT, WIDTH), lambda i, t: (i, 0, t)),
        ],
        out_specs=pl.BlockSpec((1, 3, 128, WIDTH), lambda i, t: (i, 0, 0, t)),
        compiler_params=pltpu.CompilerParams(vmem_limit_bytes=48 << 20),
    )(row_points, a, b)


def shards(spectra, legendre_table, m_order, row_points):
    spectra = spectra.reshape(WAVES, 2 * FL, DEG)
    a, b = move(spectra, legendre_table, m_order, row_points)
    return synthesize(a, b, row_points)


def solution(mesh):
    in_specs = (P("wave", None, None, "lev", None), P("wave", None, None), P(), P())
    out_specs = P(("wave", "lev"), None, None, None)
    return jax.shard_map(shards, mesh=mesh, in_specs=in_specs, out_specs=out_specs, check_vma=False)
```

time: 378 us -> 91.7 us (0.24)
  other arithmetic: 195 us -> 0 us
  Pallas kernels: 0 us -> 89.6 us
  local copies, waits for them, and re-layouts: 77.8 us -> 1.54 us
  blocking collectives: 61.1 us -> 0 us
  waiting for transfers between devices: 23.5 us -> 0 us
  matrix products: 11.3 us -> 0 us
  starting transfers between devices: 4.18 us -> 0 us
  loops' own time: 3.81 us -> 0 us
    convert_element_type x2 -> x0, other arithmetic: 192 us -> none  [synthesis_basis(): cosine = (factor * jnp.cos(angle)).astype(jnp.bfloat16)]
    pallas_call x0 -> x2, Pallas kernels: none -> 89.6 us  [the longest x1 73.8 us: move(): pl.pallas_call(move_kernel, out_shape=(jax.ShapeDtypeStruct((2, 4 * FL, K...]
    all_to_all x1 -> x0, blocking collectives: 61.1 us -> none  [shards(): lax.all_to_all(coeffs, 'wave', split_axis=0, concat_axis=2, tiled=True)]
    unnamed x4, local copies, waits for them, and re-layouts: 33.4 us -> 1.54 us
    all_to_all x1 -> x0, waiting for transfers between devices: 23.5 us -> none  [shards(): lax.all_to_all(lax.all_to_all(coeffs, 'wave', split_axis=0, concat_axis=2...]
    all_to_all x4 -> x0, local copies, waits for them, and re-layouts: 22.9 us -> none  [the longest x3 19.7 us: shards(): lax.all_to_all(coeffs, 'wave', split_axis=0, concat_axis=2, tiled=True)]
    convert_element_type x1 -> x0, local copies, waits for them, and re-layouts: 12 us -> none  [shards(): coeffs = coeffs.astype(jnp.bfloat16)]
    dot_general x3 -> x0, matrix products: 11.3 us -> none  [the longest x2 6.02 us: contract_first(): lax.dot_general(left, right, (((0,), (0,)), ((), ())), preferred_element_...]
  transfers between devices with their start and end apart: 1 -> 0, of which waited for: 1 -> 0; matrix products, arithmetic and copies ran while one was open for 0% -> 0% of each run, Pallas kernels for 0% -> 0%
where the time goes in v1:
time: 91.7 us; the launch traced here: 91.2 us
  Pallas kernels  89.6 us (98%)
  local copies, waits for them, and re-layouts  1.54 us (2%)
    pallas_call x1, Pallas kernels, move(): pl.pallas_call(move_kernel, out_shape=(jax.ShapeDtypeStruct((2, 4 * FL, K...  73.8 us
    pallas_call x1, Pallas kernels, synthesize(): pl.pallas_call(synth_kernel, out_shape=jax.ShapeDtypeStruct((2, 3, 128, R...  15.8 us

profile of v1, /device:TPU:1, one launch (start us, length us, event | category | flops | bytes accessed | tf_op | source)
XLA Modules:
  0.0 91.2 jit_solution(1929894078369516028)
XLA Ops:
  0.0 0.0 copy-start.1
  0.0 73.8 %shard_map.73 = (bf16[2,384,1280]{2,1,0:T(8,128)(2,1)}, bf16[2,1280,2688]{2,1,0:T(8,128)(2,1)}) custom-call(s32[640]{0:T(1024)} %m_ref.1, s32[512]{0:T(512)} %p_ref.3, bf16[10,192,640]{2,1,0:T(8,128)(2,1)} %bitcast.1, bf16[10,640,512]{2,1,0:T(8,128)(2,1)} %leg_hbm.1, bf16[512,512]{1,0:T(8,128)(2,1)} %constant.6.clone.by_peer_hbm, ...), custom_call_target="tpu_custom_call" | custom-call | tf_op jit(solution)/shard_map/pallas_call | solution.py:294
  73.8 0.0 copy-done.1
  73.8 0.0 copy-start
  73.8 1.5 %copy-done = bf16[2,384,1280]{2,1,0:T(8,128)(2,1)S(1)} copy-done((bf16[2,384,1280]{2,1,0:T(8,128)(2,1)S(1)}, bf16[2,384,1280]{2,1,0:T(8,128)(2,1)}, u32[]{:S(2)}) %copy-start) | copy-done | bytes 1966104
  75.4 15.8 %shard_map.74 = bf16[2,3,128,2688]{3,2,1,0:T(8,128)(2,1)} custom-call(s32[512]{0:T(512)S(1)} %copy-done.1, bf16[2,384,1280]{2,1,0:T(8,128)(2,1)S(1)} %copy-done, bf16[2,1280,2688]{2,1,0:T(8,128)(2,1)} %get-tuple-element.8.b_ref), custom_call_target="tpu_custom_call" | custom-call | tf_op jit(solution)/shard_map/pallas_call | solution.py:346
Async XLA Ops:
  0.0 73.8 %copy-start.1 = (s32[512]{0:T(512)S(1)}, s32[512]{0:T(512)}, u32[]{:S(2)}) copy-start(s32[512]{0:T(512)} %p_ref.3) | copy-start | bytes 6148
  73.8 1.5 %copy-start = (bf16[2,384,1280]{2,1,0:T(8,128)(2,1)S(1)}, bf16[2,384,1280]{2,1,0:T(8,128)(2,1)}, u32[]{:S(2)}) copy-start(bf16[2,384,1280]{2,1,0:T(8,128)(2,1)} %get-tuple-element.7.a_ref) | copy-start | bytes 5898244

commit v2 on v1

--- a/solution.py
+++ b/solution.py
@@ -39,9 +39,10 @@
     for s in range(8):
         for z in range(NZ):
             for i in range(2):
+                wave = (s // 2 * NZ + z) * NC + s % 2
                 by_z[z * 16 + i * 8 + s, s * 16 + z * 2 + i] = 1
-                to_k[z * 16 + i * 8 + s, i * 64 + z * 8 + s] = 1
-                to_k[z * 16 + i * 8 + s, 128 + (1 - i) * 64 + z * 8 + s] = 1
+                to_k[z * 16 + i * 8 + s, i * 64 + wave] = 1
+                to_k[z * 16 + i * 8 + s, 128 + (1 - i) * 64 + wave] = 1
     return tuple(jnp.asarray(a, jnp.bfloat16) for a in (by_peer, by_z, to_k))
 
 
@@ -70,10 +71,10 @@
 
 def move_kernel(
     m_ref, p_ref, spec_hbm, leg_hbm, by_peer_hbm, by_z_hbm, to_k_hbm,
-    a_hbm, b_hbm,
+    grid_hbm,
     spec, leg, by_peer, by_z, to_k, coef, sent, mid, ordered, final, a_out,
-    waves, cos_now, sin_now, cos_step, sin_step, b_out,
-    in_sem, xy_send, xy_recv, xy_own, z_send, z_recv, z_own, a_sem, b_sem,
+    waves, basis, total, grid,
+    in_sem, xy_send, xy_recv, xy_own, z_send, z_recv, z_own, grid_sem,
 ):
     w, y = lax.axis_index("wave"), lax.axis_index("lev")
     x, z, c = w // 16, lax.rem(w // 2, 8), lax.rem(w, 2)
@@ -205,83 +206,111 @@
                 a_out[0, group * FL:(group + 1) * FL, at:at + 128] = even.astype(jnp.bfloat16)
                 a_out[1, group * FL:(group + 1) * FL, at:at + 128] = odd.astype(jnp.bfloat16)
 
-    def a_copy(g):
-        cut = pl.ds(g * 256, 256)
-        return pltpu.make_async_copy(a_out.at[:, :, cut], a_hbm.at[:, :, cut], a_sem.at[g])
-
-    def b_copy(i, k, t):
-        return pltpu.make_async_copy(b_out.at[k], b_hbm.at[i, :, pl.ds(pl.multiple_of(t * 128, 128), 128)], b_sem.at[k])
-
-    def bases():
-        @pl.loop(0, KTOT // 2)
+    def gather_waves():
+        @pl.loop(0, KTOT // 2 // WAVES)
         def _(k):
-            block, s = k // 64, lax.rem(k, 8)
-            source = wave_of(s // 2, lax.rem(k // 8, 8), lax.rem(s, 2))
-            waves[pl.ds(k, 1), :] = jnp.full((1, 128), m_ref[source * WAVES + block]).astype(jnp.float32)
-
+            for block in range(WAVES):
+                waves[pl.ds(block * 64 + k, 1), :] = jnp.full((1, 128), m_ref[k * WAVES + block]).astype(jnp.float32)
+
+    def make_basis(i, block):
+        points = jnp.full((64, 128), p_ref[(w * NY + y) * 2 + i]).astype(jnp.float32)
+        wave = waves[block * 64:(block + 1) * 64, :]
+        lon = lax.broadcasted_iota(jnp.int32, (64, 128), 1).astype(jnp.float32)
+        weight = jnp.where(2.0 * wave < points, jnp.where(wave == 0.0, 1.0, 2.0), 0.0)
+        cosine, sine = unit_circle(wave, lon, points)
+        cos_step, sin_step = unit_circle(wave, 128.0, points)
+        first = block * 128 + i * 64
+        second = block * 128 + (1 - i) * 64
+
+        def step(t, now):
+            cosine, sine = now
+            cut = pl.ds(pl.multiple_of(t * 128, 128), 128)
+            basis[i, first:first + 64, cut] = cosine.astype(jnp.bfloat16)
+            basis[i, second:second + 64, cut] = sine.astype(jnp.bfloat16)
+            return cosine * cos_step + sine * sin_step, sine * cos_step - cosine * sin_step
+
+        lax.fori_loop(0, TILES, step, (weight * cosine, -weight * sine))
+
+    def bases(lo, hi):
+        for n in range(lo, hi):
+            make_basis(n % 2, n // 2)
+
+    def multiply(g):
+        k = slice(g * 256, (g + 1) * 256)
         for i in range(2):
-            count = p_ref[(w * NY + y) * 2 + i]
-
-            @pl.loop(0, 10)
-            def _(block):
-                rows = pl.ds(pl.multiple_of(block * 64, 64), 64)
-                points = jnp.full((64, 128), count).astype(jnp.float32)
-                wave = waves[rows, :]
-                lon = lax.broadcasted_iota(jnp.int32, (64, 128), 1).astype(jnp.float32)
-                cosine, sine = unit_circle(wave, lon, points)
-                weight = jnp.where(2.0 * wave < points, jnp.where(wave == 0.0, 1.0, 2.0), 0.0)
-                cos_now[rows, :] = weight * cosine
-                sin_now[rows, :] = -weight * sine
-                cosine, sine = unit_circle(wave, 128.0, points)
-                cos_step[rows, :] = cosine
-                sin_step[rows, :] = sine
-
-            @pl.loop(0, TILES)
+            def part(cut):
+                total[i, :, cut] = dot(a_out[i, :, k], basis[i, k, cut], ((1,), (0,))) + (total[i, :, cut] if g else 0.0)
+
+            @pl.loop(0, 5)
             def _(t):
-                k = lax.rem(t + i * TILES, 2)
-
-                @pl.when(t + i * TILES >= 2)
-                def _():
-                    b_copy(i, k, t).wait()
-
-                for block in range(10):
-                    rows = slice(block * 64, (block + 1) * 64)
-                    cosine, sine, cs, ss = cos_now[rows, :], sin_now[rows, :], cos_step[rows, :], sin_step[rows, :]
-                    first = block * 128 + i * 64
-                    second = block * 128 + (1 - i) * 64
-                    b_out[k, first:first + 64, :] = cosine.astype(jnp.bfloat16)
-                    b_out[k, second:second + 64, :] = sine.astype(jnp.bfloat16)
-                    cos_now[rows, :] = cosine * cs + sine * ss
-                    sin_now[rows, :] = sine * cs - cosine * ss
-                b_copy(i, k, t).start()
-
-        for k in range(2):
-            b_copy(1, k, 0).wait()
+                part(pl.ds(pl.multiple_of(t * 512, 512), 512))
+
+            part(pl.ds(2560, 128))
+
+    def grid_copy(i, t):
+        cut = pl.ds(t * 384, 384)
+        return pltpu.make_async_copy(grid.at[i, :, :, cut], grid_hbm.at[i, :, :, cut], grid_sem.at[i * 7 + t])
+
+    def finish(g):
+        k = slice(g * 256, (g + 1) * 256)
+        for i in range(2):
+            points = p_ref[(w * NY + y) * 2 + i]
+            for t in range(7):
+                cut = slice(t * 384, (t + 1) * 384)
+                field = dot(a_out[i, :, k], basis[i, k, cut], ((1,), (0,))) + total[i, :, cut]
+                lon = lax.broadcasted_iota(jnp.int32, (4 * FL, 384), 1) + t * 384
+                field = jnp.where(lon < points, field, 0.0).astype(jnp.bfloat16)
+                for group in range(NY):
+                    for f in range(3):
+                        at = group * FL + f * 32
+                        grid[i, f, group * 32:(group + 1) * 32, cut] = field[at:at + 32]
+                grid_copy(i, t).start()
 
     spectral(0)
     pl.semaphore_wait(barrier, NPEER - 1 + NZ - 1)
     send_xy(0)
     send_xy(1)
-    for g in range(1, PAIRS):
-        spectral(g)
-        send_xy(g + 1)
-    for q in range(len(PARTS)):
-        wait_xy(q)
-        send_z(q)
-    bases()
-    for q in range(len(PARTS)):
-        wait_z(q)
-        if q:
-            rows_of(q - 1)
-            a_copy(q - 1).start()
+    spectral(1)
+    send_xy(2)
+    wait_xy(0)
+    send_z(0)
+    spectral(2)
+    send_xy(3)
+    wait_xy(1)
+    send_z(1)
+    spectral(3)
+    send_xy(4)
+    spectral(4)
+    send_xy(5)
+    gather_waves()
+    bases(0, 4)
+    wait_xy(2)
+    send_z(2)
+    bases(4, 8)
+    wait_xy(3)
+    send_z(3)
+    bases(8, 14)
+    wait_xy(4)
+    send_z(4)
+    bases(14, 20)
+    wait_xy(5)
+    send_z(5)
+    wait_z(0)
     for g in range(PAIRS):
-        a_copy(g).wait()
+        wait_z(g + 1)
+        rows_of(g)
+        if g < PAIRS - 1:
+            multiply(g)
+    finish(PAIRS - 1)
     for q in range(len(PARTS)):
         first, size = PARTS[q]
         most = mid.at[pl.ds(0, NPEER - 1), :, pl.ds(first, size)]
         pltpu.make_async_copy(most, most, xy_send.at[q]).wait()
         most = final.at[pl.ds(0, NZ - 1), :, :, pl.ds(first, size)]
         pltpu.make_async_copy(most, most, z_send.at[q]).wait()
+    for i in range(2):
+        for t in range(7):
+            grid_copy(i, t).wait()
 
 
 def move(spectra, legendre_table, m_order, row_points):
@@ -293,12 +322,9 @@
     dma = pltpu.SemaphoreType.DMA
     return pl.pallas_call(
         move_kernel,
-        out_shape=(
-            jax.ShapeDtypeStruct((2, 4 * FL, KTOT), bf16),
-            jax.ShapeDtypeStruct((2, KTOT, ROWPAD), bf16),
-        ),
+        out_shape=jax.ShapeDtypeStruct((2, 3, 128, ROWPAD), bf16),
         in_specs=[smem, smem, hbm, hbm, hbm, hbm, hbm],
-        out_specs=(hbm, hbm),
+        out_specs=hbm,
         scratch_shapes=[
             pltpu.VMEM((WAVES, 2 * FL, DEG), bf16),
             pltpu.VMEM((WAVES, DEG, NLAT), bf16),
@@ -312,15 +338,13 @@
             pltpu.VMEM((NZ, NY, 16, LANES), bf16),
             pltpu.VMEM((2, 4 * FL, KTOT), bf16),
             pltpu.VMEM((KTOT // 2, 128), f32),
-            pltpu.VMEM((KTOT // 2, 128), f32),
-            pltpu.VMEM((KTOT // 2, 128), f32),
-            pltpu.VMEM((KTOT // 2, 128), f32),
-            pltpu.VMEM((KTOT // 2, 128), f32),
-            pltpu.VMEM((2, KTOT, 128), bf16),
+            pltpu.VMEM((2, KTOT, ROWPAD), bf16),
+            pltpu.VMEM((2, 4 * FL, ROWPAD), f32),
+            pltpu.VMEM((2, 3, 128, ROWPAD), bf16),
             dma((3 + 2 * PAIRS,)),
             dma((n,)), dma((n,)), dma((n,)),
             dma((n,)), dma((n,)), dma((n,)),
-            dma((PAIRS,)), dma((2,)),
+            dma((14,)),
         ],
         compiler_params=pltpu.CompilerParams(
             collective_id=0, has_side_effects=True, vmem_limit_bytes=56 << 20
@@ -328,39 +352,9 @@
     )(m_order, row_points, spectra, legendre_table, by_peer, by_z, to_k)
 
 
-WIDTH = 384
-
-
-def synth_kernel(p_ref, a_ref, b_ref, grid_ref):
-    i, t = pl.program_id(0), pl.program_id(1)
-    row = (lax.axis_index("wave") * NY + lax.axis_index("lev")) * 2 + i
-    field = dot(a_ref[0], b_ref[0], ((1,), (0,)))
-    lon = lax.broadcasted_iota(jnp.int32, (4 * FL, WIDTH), 1) + t * WIDTH
-    field = jnp.where(lon < p_ref[row], field, 0.0).astype(jnp.bfloat16)
-    for y in range(NY):
-        for f in range(3):
-            grid_ref[0, f, y * 32:(y + 1) * 32, :] = field[y * FL + f * 32:y * FL + (f + 1) * 32]
-
-
-def synthesize(a, b, row_points):
-    return pl.pallas_call(
-        synth_kernel,
-        out_shape=jax.ShapeDtypeStruct((2, 3, 128, ROWPAD), jnp.bfloat16),
-        grid=(2, ROWPAD // WIDTH),
-        in_specs=[
-            pl.BlockSpec(memory_space=pltpu.SMEM),
-            pl.BlockSpec((1, 4 * FL, KTOT), lambda i, t: (i, 0, 0)),
-            pl.BlockSpec((1, KTOT, WIDTH), lambda i, t: (i, 0, t)),
-        ],
-        out_specs=pl.BlockSpec((1, 3, 128, WIDTH), lambda i, t: (i, 0, 0, t)),
-        compiler_params=pltpu.CompilerParams(vmem_limit_bytes=48 << 20),
-    )(row_points, a, b)
-
-
 def shards(spectra, legendre_table, m_order, row_points):
     spectra = spectra.reshape(WAVES, 2 * FL, DEG)
-    a, b = move(spectra, legendre_table, m_order, row_points)
-    return synthesize(a, b, row_points)
+    return move(spectra, legendre_table, m_order, row_points)
 
 
 def solution(mesh):

time: 91.7 us -> 69.9 us (0.76)
  Pallas kernels: 89.6 us -> 65.3 us
  local copies, waits for them, and re-layouts: 1.54 us -> 4.47 us
    pallas_call x2 -> x1, Pallas kernels: 89.6 us -> 65.3 us  [move(): pl.pallas_call(move_kernel, out_shape=jax.ShapeDtypeStruct((2, 3, 128, RO...]
    unnamed x4 -> x1, local copies, waits for them, and re-layouts: 1.54 us -> 4.47 us
where the time goes in v2:
time: 69.9 us; the launch traced here: 69.8 us
  Pallas kernels  65.3 us (93%)
  local copies, waits for them, and re-layouts  4.47 us (6%)
    pallas_call x1, Pallas kernels, move(): pl.pallas_call(move_kernel, out_shape=jax.ShapeDtypeStruct((2, 3, 128, RO...  65.3 us
    unnamed x1, local copies, waits for them, and re-layouts  4.47 us

profile of v2, /device:TPU:1, one launch (start us, length us, event | category | flops | bytes accessed | tf_op | source)
XLA Modules:
  0.0 69.8 jit_solution(11190882182346552050)
XLA Ops:
  0.0 65.3 %shard_map.73 = bf16[2,3,128,2688]{3,2,1,0:T(8,128)(2,1)} custom-call(s32[640]{0:T(1024)} %m_ref.1, s32[512]{0:T(512)} %p_ref.1, bf16[10,192,640]{2,1,0:T(8,128)(2,1)} %bitcast.1, bf16[10,640,512]{2,1,0:T(8,128)(2,1)} %leg_hbm.1, bf16[512,512]{1,0:T(8,128)(2,1)} %constant.6.clone.by_peer_hbm, bf16[128,128]{1,0:T(8,128)(2,1)} %constant.7.clone.by_z_hbm, ...), custom_call_target="tpu_custom_call" | custom-call | tf_op jit(solution)/shard_map/pallas_call | solution.py:323
  65.3 4.5 %copy.9 = bf16[2,3,128,2688]{3,2,1,0:T(8,128)(2,1)} copy(bf16[2,3,128,2688]{3,2,1,0:T(8,128)(2,1)} %shard_map.73) | data formatting | bytes 8257536

commit v3 on v2

--- a/solution.py
+++ b/solution.py
@@ -22,7 +22,7 @@
 ROWPAD = 2688
 TILES = ROWPAD // 128
 KTOT = 1280
-PARTS = ((0, 128), (128, 256), (384, 384), (768, 384), (1152, 384), (1536, 384))
+PARTS = ((0, 384), (384, 128), (512, 256), (768, 384), (1152, 384), (1536, 384))
 
 
 def permutations():
@@ -71,17 +71,29 @@
 
 def move_kernel(
     m_ref, p_ref, spec_hbm, leg_hbm, by_peer_hbm, by_z_hbm, to_k_hbm,
-    grid_hbm,
-    spec, leg, by_peer, by_z, to_k, coef, sent, mid, ordered, final, a_out,
-    waves, basis, total, grid,
-    in_sem, xy_send, xy_recv, xy_own, z_send, z_recv, z_own, grid_sem,
+    total, a_last, basis_last,
+    spec, leg, by_peer, by_z, to_k, coef, sent, mid, ordered, final, a_now,
+    waves, basis,
+    in_sem, xy_send, xy_recv, xy_own, z_send, z_recv, z_own,
 ):
     w, y = lax.axis_index("wave"), lax.axis_index("lev")
     x, z, c = w // 16, lax.rem(w // 2, 8), lax.rem(w, 2)
 
-    def peer(d):
-        px, py, pc = lax.rem(x + d // 8, NX), lax.rem(y + lax.rem(d // 2, 4), NY), lax.rem(c + lax.rem(d, 2), NC)
-        return px, py, pc
+    ys = [lax.rem(y + d, NY) for d in range(NY)]
+
+    def each_peer(act):
+        @pl.loop(0, NX)
+        def _(d):
+            px = lax.rem(x + d, NX)
+
+            @pl.when(d > 0)
+            def _():
+                act(px, y, c)
+
+            for py in ys[1:]:
+                act(px, py, c)
+            for py in ys:
+                act(px, py, 1 - c)
 
     def wave_of(px, pz, pc):
         return (px * NZ + pz) * NC + pc
@@ -108,10 +120,10 @@
 
     barrier = pltpu.get_barrier_semaphore()
 
-    @pl.loop(1, NPEER)
-    def _(d):
-        px, py, pc = peer(d)
+    def greet(px, py, pc):
         pl.semaphore_signal(barrier, inc=1, device_id=(wave_of(px, z, pc), py), device_id_type=MESH)
+
+    each_peer(greet)
 
     @pl.loop(1, NZ)
     def _(d):
@@ -138,9 +150,7 @@
         first, size = PARTS[q]
         cut = pl.ds(first, size)
 
-        @pl.loop(1, NPEER)
-        def _(d):
-            px, py, pc = peer(d)
+        def send(px, py, pc):
             pltpu.make_async_remote_copy(
                 src_ref=sent.at[(px * NY + py) * NC + pc, :, cut],
                 dst_ref=mid.at[slot, :, cut],
@@ -150,6 +160,7 @@
                 device_id_type=MESH,
             ).start()
 
+        each_peer(send)
         pltpu.make_async_copy(sent.at[own, :, cut], mid.at[slot, :, cut], xy_own.at[q]).start()
 
     def wait_xy(q):
@@ -177,12 +188,14 @@
         cut = pl.ds(first, size)
         return pltpu.make_async_copy(ordered.at[z, :, :, cut], final.at[z, :, :, cut], z_own.at[q])
 
-    def send_z(q):
+    def order_z(q, rows):
         first, size = PARTS[q]
         for group in range(NY):
-            block = mid[group * 8:(group + 1) * 8, :, first:first + size].reshape(128, size)
+            block = rows[group * 8:(group + 1) * 8, :, first:first + size].reshape(128, size)
             moved = dot(by_z[...], block, ((1,), (0,))).astype(jnp.bfloat16)
             ordered[:, group, :, first:first + size] = moved.reshape(NZ, 16, size)
+
+    def send_z(q):
         for d in (4, 3, 5, 2, 6, 1, 7):
             z_copy(q, d).start()
         z_stay(q).start()
@@ -193,18 +206,29 @@
         pltpu.make_async_copy(most, most, z_recv.at[q]).wait()
         z_stay(q).wait()
 
+    def order_xy(q):
+        first, size = PARTS[q]
+        for px in range(NX):
+            block = final[:, px, :, first:first + size].reshape(128, size)
+            moved = dot(by_z[...], block, ((0,), (0,))).astype(jnp.bfloat16)
+            sent[px * 8:(px + 1) * 8, :, first:first + size] = moved.reshape(8, 16, size)
+
     def rows_of(g):
         lane = lax.broadcasted_iota(jnp.int32, (FL, 128), 1)
         for group in range(NY):
-            block = final[:, group, :, g * PAIR_LANES:(g + 1) * PAIR_LANES].reshape(128, PAIR_LANES)
+            if g == 0:
+                block = mid[group * 8:(group + 1) * 8, :, :PAIR_LANES].reshape(128, PAIR_LANES)
+                block = dot(by_z[...], block, ((1,), (0,))).astype(jnp.bfloat16)
+            else:
+                block = final[:, group, :, g * PAIR_LANES:(g + 1) * PAIR_LANES].reshape(128, PAIR_LANES)
             turned = dot(block, to_k[...], ((0,), (0,)))
             for h in range(2):
                 real, imag = (turned[(2 * h + k) * FL:(2 * h + k + 1) * FL] for k in range(2))
                 even = jnp.where(lane < 64, real[:, :128], imag[:, 128:])
                 odd = jnp.where(lane < 64, imag[:, 128:], real[:, :128])
-                at = (2 * g + h) * 128
-                a_out[0, group * FL:(group + 1) * FL, at:at + 128] = even.astype(jnp.bfloat16)
-                a_out[1, group * FL:(group + 1) * FL, at:at + 128] = odd.astype(jnp.bfloat16)
+                to = a_last if g == PAIRS - 1 else a_now
+                to[0, group * FL:(group + 1) * FL, h * 128:(h + 1) * 128] = even.astype(jnp.bfloat16)
+                to[1, group * FL:(group + 1) * FL, h * 128:(h + 1) * 128] = odd.astype(jnp.bfloat16)
 
     def gather_waves():
         @pl.loop(0, KTOT // 2 // WAVES)
@@ -219,14 +243,15 @@
         weight = jnp.where(2.0 * wave < points, jnp.where(wave == 0.0, 1.0, 2.0), 0.0)
         cosine, sine = unit_circle(wave, lon, points)
         cos_step, sin_step = unit_circle(wave, 128.0, points)
-        first = block * 128 + i * 64
-        second = block * 128 + (1 - i) * 64
+        to, at = (basis_last, block - 8) if block >= 8 else (basis, block)
+        first = at * 128 + i * 64
+        second = at * 128 + (1 - i) * 64
 
         def step(t, now):
             cosine, sine = now
             cut = pl.ds(pl.multiple_of(t * 128, 128), 128)
-            basis[i, first:first + 64, cut] = cosine.astype(jnp.bfloat16)
-            basis[i, second:second + 64, cut] = sine.astype(jnp.bfloat16)
+            to[i, first:first + 64, cut] = cosine.astype(jnp.bfloat16)
+            to[i, second:second + 64, cut] = sine.astype(jnp.bfloat16)
             return cosine * cos_step + sine * sin_step, sine * cos_step - cosine * sin_step
 
         lax.fori_loop(0, TILES, step, (weight * cosine, -weight * sine))
@@ -239,7 +264,7 @@
         k = slice(g * 256, (g + 1) * 256)
         for i in range(2):
             def part(cut):
-                total[i, :, cut] = dot(a_out[i, :, k], basis[i, k, cut], ((1,), (0,))) + (total[i, :, cut] if g else 0.0)
+                total[i, :, cut] = dot(a_now[i], basis[i, k, cut], ((1,), (0,))) + (total[i, :, cut] if g else 0.0)
 
             @pl.loop(0, 5)
             def _(t):
@@ -247,70 +272,55 @@
 
             part(pl.ds(2560, 128))
 
-    def grid_copy(i, t):
-        cut = pl.ds(t * 384, 384)
-        return pltpu.make_async_copy(grid.at[i, :, :, cut], grid_hbm.at[i, :, :, cut], grid_sem.at[i * 7 + t])
-
-    def finish(g):
-        k = slice(g * 256, (g + 1) * 256)
-        for i in range(2):
-            points = p_ref[(w * NY + y) * 2 + i]
-            for t in range(7):
-                cut = slice(t * 384, (t + 1) * 384)
-                field = dot(a_out[i, :, k], basis[i, k, cut], ((1,), (0,))) + total[i, :, cut]
-                lon = lax.broadcasted_iota(jnp.int32, (4 * FL, 384), 1) + t * 384
-                field = jnp.where(lon < points, field, 0.0).astype(jnp.bfloat16)
-                for group in range(NY):
-                    for f in range(3):
-                        at = group * FL + f * 32
-                        grid[i, f, group * 32:(group + 1) * 32, cut] = field[at:at + 32]
-                grid_copy(i, t).start()
+    def pass_on(q):
+        wait_xy(q)
+        order_z(q, mid)
+        send_z(q)
 
     spectral(0)
+    order_z(0, sent)
     pl.semaphore_wait(barrier, NPEER - 1 + NZ - 1)
-    send_xy(0)
+    send_z(0)
+    spectral(1)
     send_xy(1)
-    spectral(1)
     send_xy(2)
-    wait_xy(0)
-    send_z(0)
     spectral(2)
     send_xy(3)
-    wait_xy(1)
-    send_z(1)
+    pass_on(1)
     spectral(3)
     send_xy(4)
+    pass_on(2)
     spectral(4)
     send_xy(5)
+    wait_z(0)
+    order_xy(0)
+    send_xy(0)
     gather_waves()
     bases(0, 4)
-    wait_xy(2)
-    send_z(2)
-    bases(4, 8)
-    wait_xy(3)
-    send_z(3)
-    bases(8, 14)
-    wait_xy(4)
-    send_z(4)
-    bases(14, 20)
-    wait_xy(5)
-    send_z(5)
-    wait_z(0)
-    for g in range(PAIRS):
+    pass_on(3)
+    bases(4, 10)
+    pass_on(4)
+    bases(10, 16)
+    pass_on(5)
+    bases(16, 20)
+    wait_xy(0)
+    rows_of(0)
+    multiply(0)
+    wait_z(1)
+    wait_z(2)
+    rows_of(1)
+    multiply(1)
+    for g in range(2, PAIRS):
         wait_z(g + 1)
         rows_of(g)
         if g < PAIRS - 1:
             multiply(g)
-    finish(PAIRS - 1)
     for q in range(len(PARTS)):
         first, size = PARTS[q]
         most = mid.at[pl.ds(0, NPEER - 1), :, pl.ds(first, size)]
         pltpu.make_async_copy(most, most, xy_send.at[q]).wait()
         most = final.at[pl.ds(0, NZ - 1), :, :, pl.ds(first, size)]
         pltpu.make_async_copy(most, most, z_send.at[q]).wait()
-    for i in range(2):
-        for t in range(7):
-            grid_copy(i, t).wait()
 
 
 def move(spectra, legendre_table, m_order, row_points):
@@ -322,9 +332,13 @@
     dma = pltpu.SemaphoreType.DMA
     return pl.pallas_call(
         move_kernel,
-        out_shape=jax.ShapeDtypeStruct((2, 3, 128, ROWPAD), bf16),
+        out_shape=(
+            pltpu.VMEM((2, 4 * FL, ROWPAD), f32),
+            pltpu.VMEM((2, 4 * FL, 256), bf16),
+            pltpu.VMEM((2, 256, ROWPAD), bf16),
+        ),
         in_specs=[smem, smem, hbm, hbm, hbm, hbm, hbm],
-        out_specs=hbm,
+        out_specs=(pl.BlockSpec(memory_space=pltpu.VMEM),) * 3,
         scratch_shapes=[
             pltpu.VMEM((WAVES, 2 * FL, DEG), bf16),
             pltpu.VMEM((WAVES, DEG, NLAT), bf16),
@@ -336,25 +350,63 @@
             pltpu.VMEM((NPEER, 16, LANES), bf16),
             pltpu.VMEM((NZ, NY, 16, LANES), bf16),
             pltpu.VMEM((NZ, NY, 16, LANES), bf16),
-            pltpu.VMEM((2, 4 * FL, KTOT), bf16),
+            pltpu.VMEM((2, 4 * FL, 256), bf16),
             pltpu.VMEM((KTOT // 2, 128), f32),
-            pltpu.VMEM((2, KTOT, ROWPAD), bf16),
-            pltpu.VMEM((2, 4 * FL, ROWPAD), f32),
-            pltpu.VMEM((2, 3, 128, ROWPAD), bf16),
+            pltpu.VMEM((2, KTOT - 256, ROWPAD), bf16),
             dma((3 + 2 * PAIRS,)),
             dma((n,)), dma((n,)), dma((n,)),
             dma((n,)), dma((n,)), dma((n,)),
-            dma((14,)),
         ],
         compiler_params=pltpu.CompilerParams(
-            collective_id=0, has_side_effects=True, vmem_limit_bytes=56 << 20
+            collective_id=0, has_side_effects=True, vmem_limit_bytes=51 << 20
         ),
     )(m_order, row_points, spectra, legendre_table, by_peer, by_z, to_k)
 
 
+CUT = 384
+CUTS = ROWPAD // CUT
+
+
+def finish_kernel(p_ref, total, a_last, basis_last, grid_hbm, grid, grid_sem):
+    row = (lax.axis_index("wave") * NY + lax.axis_index("lev")) * 2
+    copies = []
+    for i in range(2):
+        points = p_ref[row + i]
+        for t in range(CUTS):
+            cut = slice(t * CUT, (t + 1) * CUT)
+            field = dot(a_last[i], basis_last[i, :, cut], ((1,), (0,))) + total[i, :, cut]
+            lon = lax.broadcasted_iota(jnp.int32, (4 * FL, CUT), 1) + t * CUT
+            field = jnp.where(lon < points, field, 0.0).astype(jnp.bfloat16)
+            for y in range(NY):
+                for f in range(3):
+                    grid[i, f, y * 32:(y + 1) * 32, cut] = field[y * FL + f * 32:y * FL + (f + 1) * 32]
+            cut = pl.ds(t * CUT, CUT)
+            copy = pltpu.make_async_copy(grid.at[i, :, :, cut], grid_hbm.at[i, :, :, cut], grid_sem.at[i * CUTS + t])
+            copy.start()
+            copies.append(copy)
+    for copy in copies:
+        copy.wait()
+
+
+def finish(total, a_last, basis_last, row_points):
+    held = pl.BlockSpec(memory_space=pltpu.VMEM)
+    return pl.pallas_call(
+        finish_kernel,
+        out_shape=jax.ShapeDtypeStruct((2, 3, 128, ROWPAD), jnp.bfloat16),
+        in_specs=[pl.BlockSpec(memory_space=pltpu.SMEM), held, held, held],
+        out_specs=pl.BlockSpec(memory_space=pl.ANY),
+        scratch_shapes=[
+            pltpu.VMEM((2, 3, 128, ROWPAD), jnp.bfloat16),
+            pltpu.SemaphoreType.DMA((2 * CUTS,)),
+        ],
+        compiler_params=pltpu.CompilerParams(vmem_limit_bytes=12 << 20),
+    )(row_points, *(pltpu.with_memory_space_constraint(v, pltpu.VMEM) for v in (total, a_last, basis_last)))
+
+
 def shards(spectra, legendre_table, m_order, row_points):
     spectra = spectra.reshape(WAVES, 2 * FL, DEG)
-    return move(spectra, legendre_table, m_order, row_points)
+    held = move(spectra, legendre_table, m_order, row_points)
+    return finish(*held, row_points)
 
 
 def solution(mesh):

time: 69.9 us -> 60.2 us (0.86)
  Pallas kernels: 65.3 us -> 60 us
  local copies, waits for them, and re-layouts: 4.47 us -> 0.01 us
    pallas_call x1 -> x2, Pallas kernels: 65.3 us -> 60 us  [the longest x1 57 us: move(): pl.pallas_call(move_kernel, out_shape=(pltpu.VMEM((2, 4 * FL, ROWPAD), f3...]
    unnamed x1 -> x2, local copies, waits for them, and re-layouts: 4.47 us -> 0.01 us
where the time goes in v3:
time: 60.2 us; the launch traced here: 60.1 us
  Pallas kernels  60 us (100%)
    pallas_call x1, Pallas kernels, move(): pl.pallas_call(move_kernel, out_shape=(pltpu.VMEM((2, 4 * FL, ROWPAD), f3...  57 us
    pallas_call x1, Pallas kernels, finish(): pl.pallas_call(finish_kernel, out_shape=jax.ShapeDtypeStruct((2, 3, 128,...  3.01 us

profile of v3, /device:TPU:1, one launch (start us, length us, event | category | flops | bytes accessed | tf_op | source)
XLA Modules:
  0.0 60.1 jit_solution(7576644716894498560)
XLA Ops:
  0.0 0.0 copy-start
  0.0 57.0 %shard_map.73 = (f32[2,384,2688]{2,1,0:T(8,128)S(1)}, bf16[2,384,256]{2,1,0:T(8,128)(2,1)S(1)}, bf16[2,256,2688]{2,1,0:T(8,128)(2,1)S(1)}) custom-call(s32[640]{0:T(1024)} %m_ref.1, s32[512]{0:T(512)} %p_ref.3, bf16[10,192,640]{2,1,0:T(8,128)(2,1)} %bitcast.1, bf16[10,640,512]{2,1,0:T(8,128)(2,1)} %leg_hbm.1, bf16[512,512]{1,0:T(8,128)(2,1)} %constant.6.clone.by_peer_hbm, ...), custom_call_target="tpu_custom_call" | custom-call | tf_op jit(solution)/shard_map/pallas_call | solution.py:333
  57.0 0.0 copy-done
  57.1 3.0 %shard_map.74 = bf16[2,3,128,2688]{3,2,1,0:T(8,128)(2,1)} custom-call(s32[512]{0:T(512)S(1)} %copy-done, f32[2,384,2688]{2,1,0:T(8,128)S(1)} %get-tuple-element.8.total, bf16[2,384,256]{2,1,0:T(8,128)(2,1)S(1)} %get-tuple-element.9.a_last, bf16[2,256,2688]{2,1,0:T(8,128)(2,1)S(1)} %get-tuple-element.10.basis_last), custom_call_target="tpu_custom_call" | custom-call | tf_op jit(solution)/shard_map/pallas_call | solution.py:393
Async XLA Ops:
  0.0 57.0 %copy-start = (s32[512]{0:T(512)S(1)}, s32[512]{0:T(512)}, u32[]{:S(2)}) copy-start(s32[512]{0:T(512)} %p_ref.3) | copy-start | bytes 6148

commit v4 on v3

--- a/solution.py
+++ b/solution.py
@@ -110,26 +110,22 @@
             pltpu.make_async_copy(spec_hbm.at[cut], spec.at[cut], in_sem.at[3 + 2 * g]),
             pltpu.make_async_copy(leg_hbm.at[cut], leg.at[cut], in_sem.at[4 + 2 * g]),
         ))
-    for f in fetch[0]:
+    for f in (*fetch[0], *loads[:2]):
         f.start()
-    for f in loads:
-        f.start()
-    for pair in fetch[1:]:
-        for f in pair:
-            f.start()
 
     barrier = pltpu.get_barrier_semaphore()
-
-    def greet(px, py, pc):
-        pl.semaphore_signal(barrier, inc=1, device_id=(wave_of(px, z, pc), py), device_id_type=MESH)
-
-    each_peer(greet)
 
     @pl.loop(1, NZ)
     def _(d):
         pl.semaphore_signal(barrier, inc=1, device_id=(wave_of(x, lax.rem(z + d, NZ), c), y), device_id_type=MESH)
 
-    for f in loads:
+    def greet(px, py, pc):
+        pl.semaphore_signal(barrier, inc=1, device_id=(wave_of(px, z, pc), py), device_id_type=MESH)
+
+    each_peer(greet)
+    for f in (*sum(fetch[1:], ()), loads[2]):
+        f.start()
+    for f in loads[:2]:
         f.wait()
     slot = y * 8 + x * 2 + c
     own = (x * NY + y) * NC + c
@@ -196,7 +192,7 @@
             ordered[:, group, :, first:first + size] = moved.reshape(NZ, 16, size)
 
     def send_z(q):
-        for d in (4, 3, 5, 2, 6, 1, 7):
+        for d in (4, 1, 7, 2, 6, 3, 5):
             z_copy(q, d).start()
         z_stay(q).start()
 
@@ -303,6 +299,7 @@
     bases(10, 16)
     pass_on(5)
     bases(16, 20)
+    loads[2].wait()
     wait_xy(0)
     rows_of(0)
     multiply(0)
@@ -363,8 +360,7 @@
     )(m_order, row_points, spectra, legendre_table, by_peer, by_z, to_k)
 
 
-CUT = 384
-CUTS = ROWPAD // CUT
+CUTS = (512, 512, 512, 512, 512, 128)
 
 
 def finish_kernel(p_ref, total, a_last, basis_last, grid_hbm, grid, grid_sem):
@@ -372,16 +368,17 @@
     copies = []
     for i in range(2):
         points = p_ref[row + i]
-        for t in range(CUTS):
-            cut = slice(t * CUT, (t + 1) * CUT)
+        for t, size in enumerate(CUTS):
+            first = sum(CUTS[:t])
+            cut = slice(first, first + size)
             field = dot(a_last[i], basis_last[i, :, cut], ((1,), (0,))) + total[i, :, cut]
-            lon = lax.broadcasted_iota(jnp.int32, (4 * FL, CUT), 1) + t * CUT
+            lon = lax.broadcasted_iota(jnp.int32, (4 * FL, size), 1) + first
             field = jnp.where(lon < points, field, 0.0).astype(jnp.bfloat16)
             for y in range(NY):
                 for f in range(3):
                     grid[i, f, y * 32:(y + 1) * 32, cut] = field[y * FL + f * 32:y * FL + (f + 1) * 32]
-            cut = pl.ds(t * CUT, CUT)
-            copy = pltpu.make_async_copy(grid.at[i, :, :, cut], grid_hbm.at[i, :, :, cut], grid_sem.at[i * CUTS + t])
+            cut = pl.ds(first, size)
+            copy = pltpu.make_async_copy(grid.at[i, :, :, cut], grid_hbm.at[i, :, :, cut], grid_sem.at[i * len(CUTS) + t])
             copy.start()
             copies.append(copy)
     for copy in copies:
@@ -397,7 +394,7 @@
         out_specs=pl.BlockSpec(memory_space=pl.ANY),
         scratch_shapes=[
             pltpu.VMEM((2, 3, 128, ROWPAD), jnp.bfloat16),
-            pltpu.SemaphoreType.DMA((2 * CUTS,)),
+            pltpu.SemaphoreType.DMA((2 * len(CUTS),)),
         ],
         compiler_params=pltpu.CompilerParams(vmem_limit_bytes=12 << 20),
     )(row_points, *(pltpu.with_memory_space_constraint(v, pltpu.VMEM) for v in (total, a_last, basis_last)))

time: 60.2 us -> 59.7 us (level)
  no operation moved by 1% of the time
where the time goes in v4:
time: 59.7 us; the launch traced here: 59.6 us
  Pallas kernels  59.6 us (100%)
    pallas_call x1, Pallas kernels, move(): pl.pallas_call(move_kernel, out_shape=(pltpu.VMEM((2, 4 * FL, ROWPAD), f3...  56.7 us
    pallas_call x1, Pallas kernels, finish(): pl.pallas_call(finish_kernel, out_shape=jax.ShapeDtypeStruct((2, 3, 128,...  2.91 us

profile of v4, /device:TPU:1, one launch (start us, length us, event | category | flops | bytes accessed | tf_op | source)
XLA Modules:
  0.0 59.6 jit_solution(7212264353790157039)
XLA Ops:
  0.0 0.0 copy-start
  0.0 56.7 %shard_map.73 = (f32[2,384,2688]{2,1,0:T(8,128)S(1)}, bf16[2,384,256]{2,1,0:T(8,128)(2,1)S(1)}, bf16[2,256,2688]{2,1,0:T(8,128)(2,1)S(1)}) custom-call(s32[640]{0:T(1024)} %m_ref.1, s32[512]{0:T(512)} %p_ref.3, bf16[10,192,640]{2,1,0:T(8,128)(2,1)} %bitcast.1, bf16[10,640,512]{2,1,0:T(8,128)(2,1)} %leg_hbm.1, bf16[512,512]{1,0:T(8,128)(2,1)} %constant.6.clone.by_peer_hbm, ...), custom_call_target="tpu_custom_call" | custom-call | tf_op jit(solution)/shard_map/pallas_call | solution.py:330
  56.7 0.0 copy-done
  56.7 2.9 %shard_map.74 = bf16[2,3,128,2688]{3,2,1,0:T(8,128)(2,1)} custom-call(s32[512]{0:T(512)S(1)} %copy-done, f32[2,384,2688]{2,1,0:T(8,128)S(1)} %get-tuple-element.8.total, bf16[2,384,256]{2,1,0:T(8,128)(2,1)S(1)} %get-tuple-element.9.a_last, bf16[2,256,2688]{2,1,0:T(8,128)(2,1)S(1)} %get-tuple-element.10.basis_last), custom_call_target="tpu_custom_call" | custom-call | tf_op jit(solution)/shard_map/pallas_call | solution.py:390
Async XLA Ops:
  0.0 56.7 %copy-start = (s32[512]{0:T(512)S(1)}, s32[512]{0:T(512)}, u32[]{:S(2)}) copy-start(s32[512]{0:T(512)} %p_ref.3) | copy-start | bytes 6148

commit v5 on v4

--- a/solution.py
+++ b/solution.py
@@ -167,12 +167,10 @@
         pltpu.make_async_copy(sent.at[own, :, cut], mid.at[slot, :, cut], xy_own.at[q]).wait()
 
     def z_copy(q, d):
-        first, size = PARTS[q]
-        cut = pl.ds(first, size)
-        pz = lax.rem(z + d, NZ)
+        pz = lax.rem(z + d + (NZ - 2 * d) * c, NZ)
         return pltpu.make_async_remote_copy(
-            src_ref=ordered.at[pz, :, :, cut],
-            dst_ref=final.at[z, :, :, cut],
+            src_ref=ordered[q].at[pz],
+            dst_ref=final[q].at[z],
             send_sem=z_send.at[q],
             recv_sem=z_recv.at[q],
             device_id=(wave_of(x, pz, c), y),
@@ -180,16 +178,14 @@
         )
 
     def z_stay(q):
-        first, size = PARTS[q]
-        cut = pl.ds(first, size)
-        return pltpu.make_async_copy(ordered.at[z, :, :, cut], final.at[z, :, :, cut], z_own.at[q])
+        return pltpu.make_async_copy(ordered[q].at[z], final[q].at[z], z_own.at[q])
 
     def order_z(q, rows):
         first, size = PARTS[q]
         for group in range(NY):
             block = rows[group * 8:(group + 1) * 8, :, first:first + size].reshape(128, size)
             moved = dot(by_z[...], block, ((1,), (0,))).astype(jnp.bfloat16)
-            ordered[:, group, :, first:first + size] = moved.reshape(NZ, 16, size)
+            ordered[q][:, group] = moved.reshape(NZ, 16, size)
 
     def send_z(q):
         for d in (4, 1, 7, 2, 6, 3, 5):
@@ -197,15 +193,14 @@
         z_stay(q).start()
 
     def wait_z(q):
-        first, size = PARTS[q]
-        most = final.at[pl.ds(0, NZ - 1), :, :, pl.ds(first, size)]
+        most = final[q].at[pl.ds(0, NZ - 1)]
         pltpu.make_async_copy(most, most, z_recv.at[q]).wait()
         z_stay(q).wait()
 
     def order_xy(q):
         first, size = PARTS[q]
         for px in range(NX):
-            block = final[:, px, :, first:first + size].reshape(128, size)
+            block = final[q][:, px].reshape(128, size)
             moved = dot(by_z[...], block, ((0,), (0,))).astype(jnp.bfloat16)
             sent[px * 8:(px + 1) * 8, :, first:first + size] = moved.reshape(8, 16, size)
 
@@ -216,7 +211,8 @@
                 block = mid[group * 8:(group + 1) * 8, :, :PAIR_LANES].reshape(128, PAIR_LANES)
                 block = dot(by_z[...], block, ((1,), (0,))).astype(jnp.bfloat16)
             else:
-                block = final[:, group, :, g * PAIR_LANES:(g + 1) * PAIR_LANES].reshape(128, PAIR_LANES)
+                here = [q for q, (first, _) in enumerate(PARTS) if first // PAIR_LANES == g]
+                block = jnp.concatenate([final[q][:, group].reshape(128, PARTS[q][1]) for q in here], axis=1)
             turned = dot(block, to_k[...], ((0,), (0,)))
             for h in range(2):
                 real, imag = (turned[(2 * h + k) * FL:(2 * h + k + 1) * FL] for k in range(2))
@@ -316,7 +312,7 @@
         first, size = PARTS[q]
         most = mid.at[pl.ds(0, NPEER - 1), :, pl.ds(first, size)]
         pltpu.make_async_copy(most, most, xy_send.at[q]).wait()
-        most = final.at[pl.ds(0, NZ - 1), :, :, pl.ds(first, size)]
+        most = final[q].at[pl.ds(0, NZ - 1)]
         pltpu.make_async_copy(most, most, z_send.at[q]).wait()
 
 
@@ -345,8 +341,8 @@
             pltpu.VMEM((PAIR_LANES, NLAT), bf16),
             pltpu.VMEM((NPEER, 16, LANES), bf16),
             pltpu.VMEM((NPEER, 16, LANES), bf16),
-            pltpu.VMEM((NZ, NY, 16, LANES), bf16),
-            pltpu.VMEM((NZ, NY, 16, LANES), bf16),
+            tuple(pltpu.VMEM((NZ, NY, 16, size), bf16) for _, size in PARTS),
+            tuple(pltpu.VMEM((NZ, NY, 16, size), bf16) for _, size in PARTS),
             pltpu.VMEM((2, 4 * FL, 256), bf16),
             pltpu.VMEM((KTOT // 2, 128), f32),
             pltpu.VMEM((2, KTOT - 256, ROWPAD), bf16),

time: 59.7 us -> 59.8 us (level)
  no operation moved by 1% of the time
where the time goes in v5:
time: 59.8 us; the launch traced here: 59.7 us
  Pallas kernels  59.6 us (100%)
    pallas_call x1, Pallas kernels, move(): pl.pallas_call(move_kernel, out_shape=(pltpu.VMEM((2, 4 * FL, ROWPAD), f3...  56.7 us
    pallas_call x1, Pallas kernels, finish(): pl.pallas_call(finish_kernel, out_shape=jax.ShapeDtypeStruct((2, 3, 128,...  2.91 us

profile of v5, /device:TPU:1, one launch (start us, length us, event | category | flops | bytes accessed | tf_op | source)
XLA Modules:
  0.0 59.7 jit_solution(6379265857829487183)
XLA Ops:
  0.0 0.0 copy-start
  0.0 56.7 %shard_map.73 = (f32[2,384,2688]{2,1,0:T(8,128)S(1)}, bf16[2,384,256]{2,1,0:T(8,128)(2,1)S(1)}, bf16[2,256,2688]{2,1,0:T(8,128)(2,1)S(1)}) custom-call(s32[640]{0:T(1024)} %m_ref.1, s32[512]{0:T(512)} %p_ref.3, bf16[10,192,640]{2,1,0:T(8,128)(2,1)} %bitcast.1, bf16[10,640,512]{2,1,0:T(8,128)(2,1)} %leg_hbm.1, bf16[512,512]{1,0:T(8,128)(2,1)} %constant.6.clone.by_peer_hbm, ...), custom_call_target="tpu_custom_call" | custom-call | tf_op jit(solution)/shard_map/pallas_call | solution.py:326
  56.7 0.0 copy-done
  56.8 2.9 %shard_map.74 = bf16[2,3,128,2688]{3,2,1,0:T(8,128)(2,1)} custom-call(s32[512]{0:T(512)S(1)} %copy-done, f32[2,384,2688]{2,1,0:T(8,128)S(1)} %get-tuple-element.8.total, bf16[2,384,256]{2,1,0:T(8,128)(2,1)S(1)} %get-tuple-element.9.a_last, bf16[2,256,2688]{2,1,0:T(8,128)(2,1)S(1)} %get-tuple-element.10.basis_last), custom_call_target="tpu_custom_call" | custom-call | tf_op jit(solution)/shard_map/pallas_call | solution.py:386
Async XLA Ops:
  0.0 56.7 %copy-start = (s32[512]{0:T(512)S(1)}, s32[512]{0:T(512)}, u32[]{:S(2)}) copy-start(s32[512]{0:T(512)} %p_ref.3) | copy-start | bytes 6148
